TPU v7x, 512 devices: a whole 4x8x8 slice. The times are simulated.
512 devices in a mesh: fsdp: 64 (over z, y_lo, core), tensor: 8 (over y_hi, x).
Axes of the slice: x: 4, y: 8 (y_hi: 2, y_lo: 4; y = y_hi * 4 + y_lo), z: 8, core: 2. Of those that a mesh axis runs over, the one named last changes fastest.
Arguments:
- grad: float32 [512, 16384], P('tensor', 'fsdp'), may hold values from -16 to 16
- basis: float32 [16384, 16384], P('fsdp', 'tensor'), may hold values from -0.046875 to 0.046875
- first_moment: float32 [512, 16384], P('fsdp', 'tensor'), may hold values from -6 to 6
- second_moment: float32 [512, 16384], P('fsdp', 'tensor'), may hold values from 0.25 to 4
Outputs:
- update: float32 [512, 16384], P('tensor', 'fsdp')
- new_first: float32 [512, 16384], P('fsdp', 'tensor')
- new_second: float32 [512, 16384], P('fsdp', 'tensor')
All inputs are finite; a program needn't handle non-finite values.
Results may differ from a plain program's by a relative error of at most 0.000076.
Values sent between devices are 32-bit elements; how exact they have to be, the bound alone decides.
A program may use at most 64 MiB of HBM per device.

v0:
```python
import jax
import jax.numpy as jnp
from jax import lax
from jax.sharding import PartitionSpec as P

STEP = 10


def moment_step(rotated, first_moment, second_moment):
    new_first = 0.9 * first_moment + 0.1 * rotated
    new_second = 0.95 * second_moment + 0.05 * rotated * rotated
    first_fix = 1.0 - 0.9**STEP
    second_fix = 1.0 - 0.95**STEP
    direction = new_first / first_fix / (jnp.sqrt(new_second / second_fix) + 1e-08)
    return (new_first, new_second, direction)


def shards(grad, basis, first_moment, second_moment):
    partial_front = jnp.dot(
        lax.all_gather(grad, "tensor", axis=0, tiled=True),
        basis,
        precision=lax.Precision.HIGHEST,
        preferred_element_type=jnp.float32,
    )
    rotated = lax.psum_scatter(partial_front, "fsdp", scatter_dimension=0, tiled=True)
    new_first, new_second, direction = moment_step(rotated, first_moment, second_moment)
    partial_back = lax.dot_general(
        lax.all_gather(direction, "fsdp", axis=0, tiled=True),
        basis,
        (((1,), (1,)), ((), ())),
        precision=lax.Precision.HIGHEST,
        preferred_element_type=jnp.float32,
    )
    update = lax.psum_scatter(partial_back, "tensor", scatter_dimension=0, tiled=True)
    return (update, new_first, new_second)


def solution(mesh):
    return jax.shard_map(
        shards,
        mesh=mesh,
        in_specs=(
            P("tensor", "fsdp"),
            P("fsdp", "tensor"),
            P("fsdp", "tensor"),
            P("fsdp", "tensor"),
        ),
        out_specs=(P("tensor", "fsdp"), P("fsdp", "tensor"), P("fsdp", "tensor")),
        check_vma=False,
    )
```

profile of v0, /device:TPU:56, one launch (start us, length us, event | category | flops | bytes accessed | tf_op | source)
XLA Modules:
  0.0 565.2 jit_solution(17410050748695483315)
XLA Ops:
  7.2 0.0 copy-start
  7.2 0.0 reduce-scatter.3.cloned.1.call-start
  7.2 45.5 %all_gather.6 = f32[512,256]{1,0:T(8,128)S(1)} all-gather(f32[64,256]{1,0:T(8,128)} %param.4), channel_id=1, replica_groups=mesh['fsdp'=64,'tensor'=8] {'tensor'}, dimensions={0}, use_global_device_ids=true | all-gather | bytes 589824 | tf_op jit(solution)/shard_map/all_gather | solution.py:20
  52.8 0.0 copy-done
  52.8 5.1 fusion.2
  57.9 0.0 copy-start.1
  57.9 0.0 copy-start.2
  57.9 0.0 reduce-scatter.3.cloned.1.call-update
  57.9 0.0 all-gather.2.cloned.1.call-start
  57.9 274.2 %reduce-scatter.3.cloned.1.call-done = f32[8,2048]{1,0:T(8,128)} async-done(((f32[512,2048]{1,0:T(8,128)}), f32[8,2048]{1,0:T(8,128)}) %reduce-scatter.3.cloned.1.call-update) | async-done | bytes 65552 | tf_op jit(solution)/shard_map/reduce_scatter | solution.py:25
  332.1 0.0 copy-done.1
  332.1 0.0 copy-done.2
  332.1 1.5 add_divide_fusion
  333.7 0.0 all-gather.2.cloned.1.call-update
  333.7 0.0 reduce-scatter.5.cloned.1.call-start
  333.7 134.4 %all-gather.2.cloned.1.call-done = f32[512,2048]{1,0:T(8,128)} async-done(((f32[8,2048]{1,0:T(8,128)}), f32[512,2048]{1,0:T(8,128)}) %all-gather.2.cloned.1.call-update) | async-done | bytes 4194320 | tf_op jit(solution)/shard_map/all_gather | solution.py:28
  468.2 6.4 %fusion.3 = f32[512,256]{1,0:T(8,128)} fusion(f32[512,2048]{1,0:T(8,128)} %all-gather.2.cloned.1.call-done, f32[256,2048]{1,0:T(8,128)S(1)} %copy-done), kind=kOutput, calls=%fused_computation.5 | convolution fusion | flops 3221225472 | bytes 6815744 | tf_op jit(solution)/shard_map/dot_general | solution.py:27
  474.6 0.0 reduce-scatter.5.cloned.1.call-update
  474.6 84.1 %reduce-scatter.5.cloned.1.call-done = f32[64,256]{1,0:T(8,128)} async-done(((f32[512,256]{1,0:T(8,128)}), f32[64,256]{1,0:T(8,128)}) %reduce-scatter.5.cloned.1.call-update) | async-done | bytes 65552 | tf_op jit(solution)/shard_map/reduce_scatter | solution.py:34
Async XLA Ops:
  7.2 45.6 %copy-start = (f32[256,2048]{1,0:T(8,128)S(1)}, f32[256,2048]{1,0:T(8,128)}, u32[]{:S(2)}) copy-start(f32[256,2048]{1,0:T(8,128)} %param.5) | copy-start | bytes 6291460
  7.2 324.9 %reduce-scatter.3.cloned.1.call-start = ((), (), s32[]{:S(2)}) async-start(), calls=%async_computation.2 | async-start | bytes 4259840 | tf_op jit(solution)/shard_map/reduce_scatter | solution.py:25
  57.9 274.3 %copy-start.1 = (f32[8,2048]{1,0:T(8,128)S(1)}, f32[8,2048]{1,0:T(8,128)}, u32[]{:S(2)}) copy-start(f32[8,2048]{1,0:T(8,128)} %param.6) | copy-start | bytes 196612
  57.9 274.3 %copy-start.2 = (f32[8,2048]{1,0:T(8,128)S(1)}, f32[8,2048]{1,0:T(8,128)}, u32[]{:S(2)}) copy-start(f32[8,2048]{1,0:T(8,128)} %param.7) | copy-start | bytes 196612
  57.9 410.3 %all-gather.2.cloned.1.call-start = ((), (), s32[]{:S(2)}) async-start(), calls=%async_computation.3 | async-start | bytes 4259840 | tf_op jit(solution)/shard_map/all_gather | solution.py:28
  333.7 225.0 %reduce-scatter.5.cloned.1.call-start = ((), (), s32[]{:S(2)}) async-start(), calls=%async_computation.4 | async-start | bytes 589824 | tf_op jit(solution)/shard_map/reduce_scatter | solution.py:34
Sparse Core Ops, SparseCore 0:
  58.0 274.0 reduce-scatter.2
  335.1 133.0 all-gather.1
  474.7 83.9 reduce-scatter.4
where the time goes:
time: 568 us; the launch traced here: 565 us
  waiting for transfers between devices  493 us (87%)
  blocking collectives  45.5 us (8%)
  between operations  13.8 us (2%)
  matrix products  11.5 us (2%)
    reduce_scatter x1, waiting for transfers between devices, shards(): lax.psum_scatter(partial_front, 'fsdp', scatter_dimension=0, tiled=True)  274 us
    all_gather x1, waiting for transfers between devices, shards(): lax.all_gather(direction, 'fsdp', axis=0, tiled=True)  134 us
    reduce_scatter x1, waiting for transfers between devices, shards(): lax.psum_scatter(partial_back, 'tensor', scatter_dimension=0, tiled=True)  84.1 us
    all_gather x1, blocking collectives, shards(): lax.all_gather(grad, 'tensor', axis=0, tiled=True)  45.5 us
  transfers between devices with their start and end apart: 3, of which 3 were waited for; matrix products, arithmetic and copies ran while one was open for 0% of the time, Pallas kernels for 0%

commit v1 on v0

v1 whole, which is shorter than its diff:
```python
import jax
import jax.numpy as jnp
from jax import lax
from jax.experimental import pallas as pl
from jax.experimental.pallas import tpu as pltpu
from jax.sharding import PartitionSpec as P

MESH = pl.DeviceIdType.MESH
F32, BF16 = jnp.float32, jnp.bfloat16
STEP = 10
C = 2048
K = 256
WA = 1536
WB = C - WA
HA, HB = WA // 2, WB // 2


def moment_step(rotated, first_moment, second_moment):
    new_first = 0.9 * first_moment + 0.1 * rotated
    new_second = 0.95 * second_moment + 0.05 * rotated * rotated
    first_fix = 1.0 - 0.9**STEP
    second_fix = 1.0 - 0.95**STEP
    direction = new_first / first_fix / (jnp.sqrt(new_second / second_fix) + 1e-08)
    return (new_first, new_second, direction)


def halves(x):
    hi = x.astype(BF16)
    return hi, (x - hi.astype(F32)).astype(BF16)


def kernel(
    grad, basis, m1, m2,
    update, nf, ns,
    own, sib, bhi, blo, g, ast, pf, ra, ya, yb, rb, d, u, xr, st, fin,
    local_sem, send, basis_sem, g_sem, ra_sem, ya_sem, yb_sem, rb_sem,
    da_sem, dya_sem, db_sem, dyb_sem, x_sem, fin_sem,
):
    f, t = lax.axis_index("fsdp"), lax.axis_index("tensor")
    z, yl, c = f // 8, (f // 2) % 4, f % 2
    yh, x = t // 4, t % 4

    def dev(dx=0, dh=0, dl=0, dz=0, dc=0):
        return (
            ((z + dz + 8) % 8) * 8 + ((yl + dl + 4) % 4) * 2 + (c + dc) % 2,
            ((yh + dh) % 2) * 4 + (x + dx + 4) % 4,
        )

    barrier = pltpu.get_barrier_semaphore()
    friends = [dev(dc=1), dev(dz=1), dev(dz=-1)]
    friends += [dev(dl=j) for j in (1, 2, 3)]
    friends += [dev(dh=1, dc=e) for e in (0, 1)]
    friends += [dev(dx=j, dc=e) for j in (1, 2, 3) for e in (0, 1)]
    for friend in friends:
        pl.semaphore_signal(barrier, inc=1, device_id=friend, device_id_type=MESH)
    load = pltpu.make_async_copy(basis, own, local_sem)
    load.start()

    started = []

    def remote(src, dst, recv_sem, to):
        return pltpu.make_async_remote_copy(
            src_ref=src, dst_ref=dst, send_sem=send.at[len(started)],
            recv_sem=recv_sem, device_id=to, device_id_type=MESH,
        )

    def put(src, dst, recv_sem, to):
        copy = remote(src, dst, recv_sem, to)
        copy.start()
        started.append(copy)

    def got(dst, recv_sem):
        pltpu.make_async_remote_copy(
            src_ref=dst, dst_ref=dst, send_sem=send.at[0],
            recv_sem=recv_sem, device_id=dev(dc=1), device_id_type=MESH,
        ).wait_recv()

    def split_basis(src, base):
        @pl.loop(0, K // 16)
        def _(i):
            hi, lo = halves(src[pl.ds(pl.multiple_of(i * 16, 16), 16), :])
            at = pl.multiple_of(base + i * 16, 16)
            bhi[pl.ds(at, 16), :] = hi
            blo[pl.ds(at, 16), :] = lo

    g[t, 0] = grad[:, c]
    load.wait()
    split_basis(own, 0)
    pl.semaphore_wait(barrier, len(friends))

    tp = ((yh + 1) % 2) * 4 + x
    for e in (0, 1):
        put(grad.at[:, (c + e) % 2], g.at[t, e], g_sem.at[1, e], dev(dh=1, dc=e))
    put(grad.at[:, 1 - c], g.at[t, 1], g_sem.at[0, 1], dev(dc=1))
    for j in (1, 3, 2):
        for e in (0, 1):
            put(grad.at[:, (c + e) % 2], g.at[t, e], g_sem.at[1 + j, e], dev(dx=j, dc=e))
    put(own, sib, basis_sem, dev(dc=1))
    for e in (0, 1):
        got(g.at[tp, e], g_sem.at[1, e])
    for j in (1, 3, 2):
        put(g.at[tp], g.at[tp], g_sem.at[4 + j, 0], dev(dx=j))
    got(sib, basis_sem)
    split_basis(sib, K)
    got(g.at[t, 1], g_sem.at[0, 1])
    for j in (1, 3, 2):
        for e in (0, 1):
            got(g.at[yh * 4 + (x + 4 - j) % 4, e], g_sem.at[1 + j, e])
    for j in (1, 3, 2):
        got(g.at[((yh + 1) % 2) * 4 + (x + 4 - j) % 4], g_sem.at[4 + j, 0])

    for e in (0, 1):
        hi, lo = halves(g[:, e].reshape(256, K))
        ast[0:256, e * K : (e + 1) * K] = hi
        ast[256:512, e * K : (e + 1) * K] = lo

    def front(i):
        cols = pl.ds(pl.multiple_of(i * 512, 512), 512)
        big = jnp.dot(ast[...], bhi[:, cols], preferred_element_type=F32)
        out = big[0:256] + big[256:512]
        out += jnp.dot(ast[0:256, :], blo[:, cols], preferred_element_type=F32)
        pf[:, :, :, cols] = out.reshape(8, 4, 8, 512)

    front(3)
    for j in (1, 2, 3):
        put(
            pf.at[:, (yl + j) % 4, :, pl.ds(WA, WB)], yb.at[j - 1],
            yb_sem.at[j - 1], dev(dl=j),
        )

    @pl.loop(0, WA // 512)
    def _(i):
        front(i)

    SIGN = (1, -1)
    order = (1, 2, 3, 0)

    def zed(k):
        return (z + k + 16) % 8

    def cut(base, half, way, s):
        return pl.ds(base + way * half, half) if s == 0 else pl.ds(base, 2 * half)

    def send_a(s, j, way):
        q, cols = (yl + j) % 4, cut(0, HA, way, s)
        put(
            pf.at[zed(SIGN[way] * (4 - s)), q, :, cols], ra.at[way, s, j, :, cols],
            ra_sem.at[way, s, j], dev(dz=SIGN[way]),
        )

    def send_b(s, way):
        put(
            pf.at[zed(SIGN[way] * (4 - s)), yl, :, cut(WA, HB, way, s)],
            rb.at[way, s, :, cut(0, HB, way, s)],
            rb_sem.at[way, s], dev(dz=SIGN[way]),
        )

    def add_a(s, j, way):
        q, cols = (yl + j) % 4, cut(0, HA, way, s)
        got(ra.at[way, s, j, :, cols], ra_sem.at[way, s, j])
        at = zed(SIGN[way] * (3 - s))
        pf[at, q, :, cols] = pf[at, q, :, cols] + ra[way, s, j, :, cols]

    def add_b(s, way):
        cols = cut(0, HB, way, s)
        got(rb.at[way, s, :, cols], rb_sem.at[way, s])
        at, to = zed(SIGN[way] * (3 - s)), cut(WA, HB, way, s)
        pf[at, yl, :, to] = pf[at, yl, :, to] + rb[way, s, :, cols]

    def step_a(s, j):
        for way in (0, 1):
            add_a(s, j, way)
            send_a(s + 1, j, way)

    def step_b(s):
        for way in (0, 1):
            add_b(s, way)
            if s < 3:
                send_b(s + 1, way)

    def last_a(j):
        for way in (0, 1):
            add_a(3, j, way)
        if j:
            put(
                pf.at[z, (yl + j) % 4, :, pl.ds(0, WA)], ya.at[j - 1],
                ya_sem.at[j - 1], dev(dl=j),
            )

    for j in order:
        for way in (0, 1):
            send_a(0, j, way)
    for s in (0, 1):
        for j in order:
            step_a(s, j)
    for j in (1, 2, 3):
        got(yb.at[j - 1], yb_sem.at[j - 1])
    bcols = pl.ds(WA, WB)
    pf[:, yl, :, bcols] = pf[:, yl, :, bcols] + yb[0] + yb[1] + yb[2]
    for way in (0, 1):
        send_b(0, way)
    step_a(2, 1)
    step_a(2, 2)
    step_b(0)
    step_a(2, 3)
    step_a(2, 0)
    step_b(1)
    last_a(1)
    last_a(2)
    step_b(2)
    last_a(3)
    step_b(3)

    def moments(rotated, base, width):
        cols = pl.ds(base, width)
        a, b, direction = moment_step(rotated, m1[:, cols], m2[:, cols])
        nf[:, cols] = a
        ns[:, cols] = b
        d[z, yl, :, cols] = direction

    def fwd_a(s, j, way):
        at, q = zed(-SIGN[way] * s), (yl + 4 - j) % 4
        cols = pl.ds(way * HA, HA) if s == 3 else pl.ds(0, WA)
        if s:
            got(d.at[at, q, :, pl.ds(0, WA)], da_sem.at[way, s - 1, j])
        put(
            d.at[at, q, :, cols], d.at[at, q, :, cols],
            da_sem.at[way, s, j], dev(dz=SIGN[way]),
        )

    def spread_b(k, n):
        at = zed(k)
        for j in (1, 2, 3):
            put(
                d.at[at, yl, :, bcols], d.at[at, yl, :, bcols],
                dyb_sem.at[n, j - 1], dev(dl=j),
            )

    def fwd_b(s):
        for way in (0, 1):
            at = zed(-SIGN[way] * s)
            cols = pl.ds(WA + way * HB, HB) if s == 3 else bcols
            if s:
                got(d.at[at, yl, :, bcols], db_sem.at[way, s - 1])
            put(
                d.at[at, yl, :, cols], d.at[at, yl, :, cols],
                db_sem.at[way, s], dev(dz=SIGN[way]),
            )
        if s:
            for way in (0, 1):
                spread_b(-SIGN[way] * s, 2 * s - 1 + way)
        else:
            spread_b(0, 0)

    moments(pf[z, yl, :, bcols], WA, WB)
    fwd_b(0)
    last_a(0)
    for j in (1, 2, 3):
        got(ya.at[j - 1], ya_sem.at[j - 1])
    moments(pf[z, yl, :, pl.ds(0, WA)] + ya[0] + ya[1] + ya[2], 0, WA)
    acols = pl.ds(0, WA)
    for way in (0, 1):
        fwd_a(0, 0, way)
    for j in (1, 2, 3):
        put(
            d.at[z, yl, :, acols], d.at[z, yl, :, acols],
            dya_sem.at[j - 1], dev(dl=j),
        )
    for j in (1, 2, 3):
        got(d.at[z, (yl + 4 - j) % 4, :, acols], dya_sem.at[j - 1])
        for way in (0, 1):
            fwd_a(0, j, way)
        if j == 1:
            fwd_b(1)
    fwd_b(2)

    def wait_b(k, n):
        for j in (1, 2, 3):
            got(d.at[zed(k), (yl + 4 - j) % 4, :, bcols], dyb_sem.at[n, j - 1])

    cond_sends = []

    def flush(n0):
        for copy, pred in cond_sends[n0:]:
            @pl.when(pred)
            def _():
                copy.start()

    def finish(k):
        tt = zed(k)
        hh = tt // 4

        @pl.when(tt % 4 == x)
        def _():
            for j in (1, 2, 3):
                got(xr.at[hh, j - 1], x_sem.at[hh, j - 1])
            total = u[tt] + xr[hh, 0] + xr[hh, 1] + xr[hh, 2]
            for e in (0, 1):
                st[hh, e] = total[:, e * K : (e + 1) * K]

            @pl.when(hh == yh)
            def _():
                final[0].start()

            @pl.when(hh != yh)
            def _():
                final[1].start()
                final[2].start()

    NS = 160
    other = (yh + 1) % 2

    def final_copy(i, src, to):
        return pltpu.make_async_remote_copy(
            src_ref=src, dst_ref=fin.at[i], send_sem=send.at[NS - 1 - i],
            recv_sem=fin_sem.at[i], device_id=to, device_id_type=MESH,
        )

    final = [
        final_copy(0, st.at[yh, 1], dev(dc=1)),
        final_copy(1, st.at[other, 0], dev(dh=1)),
        final_copy(2, st.at[other, 1], dev(dh=1, dc=1)),
    ]
    SB = 144

    def back(ks):
        n0 = len(cond_sends)
        rows = 32 * len(ks)
        parts = [d[zed(k)].reshape(32, C) for k in ks]
        hi, lo = halves(jnp.concatenate(parts, 0) if len(ks) > 1 else parts[0])
        nt = (((1,), (1,)), ((), ()))
        big = lax.dot_general(
            jnp.concatenate([hi, lo], 0), bhi[...], nt, preferred_element_type=F32
        )
        out = big[0:rows] + big[rows : 2 * rows]
        out += lax.dot_general(hi, blo[...], nt, preferred_element_type=F32)
        for i, k in enumerate(ks):
            u[zed(k)] = out[32 * i : 32 * i + 32]
        for k in ks:
            tt = zed(k)
            xx, hh = tt % 4, tt // 4
            slot = (xx + 3 - x + 4) % 4
            slot = jnp.minimum(slot, 2)
            copy = pltpu.make_async_remote_copy(
                src_ref=u.at[tt], dst_ref=xr.at[hh, slot],
                send_sem=send.at[SB + len(cond_sends)],
                recv_sem=x_sem.at[hh, slot],
                device_id=(f, yh * 4 + xx), device_id_type=MESH,
            )
            cond_sends.append((copy, xx != x))
        flush(n0)

    for j in (0, 1):
        for way in (0, 1):
            fwd_a(1, j, way)
    fwd_b(3)
    for j in (2, 3):
        for way in (0, 1):
            fwd_a(1, j, way)
    for way in (0, 1):
        half = pl.ds(WA + way * HB, HB)
        got(d.at[zed(4), yl, :, half], db_sem.at[way, 3])
    spread_b(4, 7)
    wait_b(0, 0)
    back([0])
    for j in range(4):
        for way in (0, 1):
            fwd_a(2, j, way)
    for way in (0, 1):
        wait_b(-SIGN[way], 1 + way)
    back([1, -1])
    finish(0)
    for j in range(4):
        for way in (0, 1):
            fwd_a(3, j, way)
    for way in (0, 1):
        wait_b(-SIGN[way] * 2, 3 + way)
    back([2, -2])
    finish(1)
    finish(-1)
    for way in (0, 1):
        wait_b(-SIGN[way] * 3, 5 + way)
    back([3, -3])
    finish(2)
    finish(-2)
    for j in range(4):
        for way in (0, 1):
            got(
                d.at[zed(4), (yl + 4 - j) % 4, :, pl.ds(way * HA, HA)],
                da_sem.at[way, 3, j],
            )
    wait_b(4, 7)
    back([4])
    finish(3)
    finish(-3)
    finish(4)

    for i in range(3):
        got(fin.at[i], fin_sem.at[i])
    update[:, c] = (st[yh, 0] + fin[1]).reshape(4, 8, K)
    update[:, 1 - c] = (fin[0] + fin[2]).reshape(4, 8, K)

    assert len(started) <= SB
    for copy in started:
        copy.wait_send()
    for copy, pred in cond_sends:
        @pl.when(pred)
        def _():
            copy.wait_send()
    for copy in final:
        copy.wait_send()


def shards(grad, basis, m1, m2):
    vmem = pl.BlockSpec(memory_space=pltpu.VMEM)
    dma = pltpu.SemaphoreType.DMA
    update, nf, ns = pl.pallas_call(
        kernel,
        out_shape=(
            jax.ShapeDtypeStruct((4, 2, 8, K), F32),
            jax.ShapeDtypeStruct((8, C), F32),
            jax.ShapeDtypeStruct((8, C), F32),
        ),
        in_specs=[vmem, pl.BlockSpec(memory_space=pl.ANY), vmem, vmem],
        out_specs=(vmem, vmem, vmem),
        scratch_shapes=[
            pltpu.VMEM((K, C), F32),
            pltpu.VMEM((K, C), F32),
            pltpu.VMEM((2 * K, C), BF16),
            pltpu.VMEM((2 * K, C), BF16),
            pltpu.VMEM((8, 2, 4, 8, K), F32),
            pltpu.VMEM((512, 2 * K), BF16),
            pltpu.VMEM((8, 4, 8, C), F32),
            pltpu.VMEM((2, 4, 4, 8, WA), F32),
            pltpu.VMEM((3, 8, WA), F32),
            pltpu.VMEM((3, 8, 8, WB), F32),
            pltpu.VMEM((2, 4, 8, WB), F32),
            pltpu.VMEM((8, 4, 8, C), F32),
            pltpu.VMEM((8, 32, 2 * K), F32),
            pltpu.VMEM((2, 3, 32, 2 * K), F32),
            pltpu.VMEM((2, 2, 32, K), F32),
            pltpu.VMEM((3, 32, K), F32),
            dma,
            dma((160,)),
            dma,
            dma((8, 2)),
            dma((2, 4, 4)),
            dma((3,)),
            dma((3,)),
            dma((2, 4)),
            dma((2, 4, 4)),
            dma((3,)),
            dma((2, 4)),
            dma((8, 3)),
            dma((2, 3)),
            dma((3,)),
        ],
        compiler_params=pltpu.CompilerParams(
            collective_id=0, has_side_effects=True, vmem_limit_bytes=48 * 2**20
        ),
        name="soap_step",
    )(grad.reshape(4, 2, 8, K), basis, m1, m2)
    return update.reshape(64, K), nf, ns


def solution(mesh):
    return jax.shard_map(
        shards,
        mesh=mesh,
        in_specs=(
            P("tensor", "fsdp"),
            P("fsdp", "tensor"),
            P("fsdp", "tensor"),
            P("fsdp", "tensor"),
        ),
        out_specs=(P("tensor", "fsdp"), P("fsdp", "tensor"), P("fsdp", "tensor")),
        check_vma=False,
    )
```

time: 568 us -> 99.9 us (0.18)
  waiting for transfers between devices: 493 us -> 0 us
  Pallas kernels: 0 us -> 92.6 us
  blocking collectives: 45.5 us -> 0 us
  between operations: 13.8 us -> 0.65 us
  matrix products: 11.5 us -> 0 us
  local copies, waits for them, and re-layouts: 0.02 us -> 5.99 us
    reduce_scatter x2 -> x0, waiting for transfers between devices: 358 us -> none  [the longest x1 274 us: shards(): lax.psum_scatter(partial_front, 'fsdp', scatter_dimension=0, tiled=True)]
    all_gather x1 -> x0, waiting for transfers between devices: 134 us -> none  [shards(): lax.all_gather(direction, 'fsdp', axis=0, tiled=True)]
    pallas_call x0 -> x1, Pallas kernels: none -> 92.6 us  [shards(): pl.pallas_call(kernel, out_shape=(jax.ShapeDtypeStruct((4, 2, 8, K), F32)...]
    all_gather x1 -> x0, blocking collectives: 45.5 us -> none  [shards(): lax.all_gather(grad, 'tensor', axis=0, tiled=True)]
    dot_general x2 -> x0, matrix products: 11.5 us -> none  [the longest x1 6.45 us: shards(): lax.dot_general(lax.all_gather(direction, 'fsdp', axis=0, tiled=True), ba...]
    unnamed x6 -> x11, local copies, waits for them, and re-layouts: 0.02 us -> 5.99 us
  transfers between devices with their start and end apart: 3 -> 0, of which waited for: 3 -> 0; matrix products, arithmetic and copies ran while one was open for 0% -> 0% of each run, Pallas kernels for 0% -> 0%
where the time goes in v1:
time: 99.9 us; the launch traced here: 99.3 us
  Pallas kernels  92.6 us (93%)
  local copies, waits for them, and re-layouts  5.99 us (6%)
    pallas_call x1, Pallas kernels, shards(): pl.pallas_call(kernel, out_shape=(jax.ShapeDtypeStruct((4, 2, 8, K), F32)...  92.6 us
    unnamed x11, local copies, waits for them, and re-layouts  5.99 us

profile of v1, /device:TPU:56, one launch (start us, length us, event | category | flops | bytes accessed | tf_op | source)
XLA Modules:
  0.0 99.3 jit_solution(5244718840958518607)
XLA Ops:
  0.6 0.0 copy-start
  0.6 1.6 %copy-done = f32[256,2048]{1,0:T(8,128)S(1)} copy-done((f32[256,2048]{1,0:T(8,128)S(1)}, f32[256,2048]{1,0:T(8,128)}, u32[]{:S(2)}) %copy-start) | copy-done | bytes 2097176
  2.2 0.0 copy-start.1
  2.2 0.8 copy-done.1
  3.1 0.0 copy-start.2
  3.1 0.8 copy-done.2
  3.9 0.0 copy-start.3
  3.9 0.8 copy-done.3
  4.7 92.6 %soap_step.1 = (f32[4,2,8,256]{3,2,1,0:T(8,128)S(1)}, f32[8,2048]{1,0:T(8,128)S(1)}, f32[8,2048]{1,0:T(8,128)S(1)}) custom-call(f32[4,2,8,256]{3,2,1,0:T(8,128)S(1)} %bitcast.2, f32[256,2048]{1,0:T(8,128)S(1)} %copy-done, f32[8,2048]{1,0:T(8,128)S(1)} %copy-done.2, f32[8,2048]{1,0:T(8,128)S(1)} %copy-done.3), custom_call_target="tpu_custom_call" | custom-call | tf_op jit(solution)/shard_map/soap_step/pallas_call | solution.py:417
  97.4 0.6 copy.10
  98.0 0.6 copy.11
  98.6 0.6 copy.12
Async XLA Ops:
  0.6 1.6 %copy-start = (f32[256,2048]{1,0:T(8,128)S(1)}, f32[256,2048]{1,0:T(8,128)}, u32[]{:S(2)}) copy-start(f32[256,2048]{1,0:T(8,128)} %basis.1) | copy-start | bytes 6291460
  2.2 0.8 copy-start.1
  3.1 0.8 copy-start.2
  3.9 0.8 copy-start.3

commit v2 on v0

v2 whole, which is shorter than its diff:
```python
import jax
import jax.numpy as jnp
from jax import lax
from jax.experimental import pallas as pl
from jax.experimental.pallas import tpu as pltpu
from jax.sharding import PartitionSpec as P

MESH = pl.DeviceIdType.MESH
F32, BF16 = jnp.float32, jnp.bfloat16
STEP = 10
C = 2048
K = 256
PARTS = ((0, 768), (768, 768))
WA = PARTS[1][0] + PARTS[1][1]
WB = C - WA
FAR = (4, 3, -3, 2, -2, 1, -1)
SB = 200


def moment_step(rotated, first_moment, second_moment):
    new_first = 0.9 * first_moment + 0.1 * rotated
    new_second = 0.95 * second_moment + 0.05 * rotated * rotated
    first_fix = 1.0 - 0.9**STEP
    second_fix = 1.0 - 0.95**STEP
    direction = new_first / first_fix / (jnp.sqrt(new_second / second_fix) + 1e-08)
    return (new_first, new_second, direction)


def halves(x):
    hi = x.astype(BF16)
    return hi, (x - hi.astype(F32)).astype(BF16)


def kernel(
    grad_hbm, basis, m1_hbm, m2_hbm,
    update_hbm, nf_hbm, ns_hbm,
    update, nf, ns, own, sib, bhi, blo, grad, m1, m2, gl, g, ast, pf, ra, ya, yb, rb, d, u, xr, st, fin,
    local_sem, send, basis_sem, g_sem, ra_sem, ya_sem, yb_sem, rb_sem,
    da_sem, dya_sem, db_sem, dyb_sem, x_sem, fin_sem,
):
    f, t = lax.axis_index("fsdp"), lax.axis_index("tensor")
    z, yl, c = f // 8, (f // 2) % 4, f % 2
    yh, x = t // 4, t % 4

    def dev(dx=0, dh=0, dl=0, dz=0, dc=0):
        return (
            ((z + dz + 8) % 8) * 8 + ((yl + dl + 4) % 4) * 2 + (c + dc) % 2,
            ((yh + dh) % 2) * 4 + (x + dx + 4) % 4,
        )

    barrier = pltpu.get_barrier_semaphore()
    friends = [dev(dh=1, dc=e) for e in (0, 1)]
    friends += [dev(dx=j, dc=e) for j in (2, 1, 3) for e in (0, 1)]
    friends += [dev(dl=j) for j in (1, 2, 3)]
    friends += [dev(dz=k) for k in FAR] + [dev(dc=1)]
    for friend in friends:
        pl.semaphore_signal(barrier, inc=1, device_id=friend, device_id_type=MESH)
    loads = [
        pltpu.make_async_copy(a, b, local_sem.at[i])
        for i, (a, b) in enumerate(
            ((grad_hbm, grad), (basis, own), (m1_hbm, m1), (m2_hbm, m2))
        )
    ]
    for copy in loads:
        copy.start()
    outs = [
        pltpu.make_async_copy(a, b, local_sem.at[4 + i])
        for i, (a, b) in enumerate(((update, update_hbm), (nf, nf_hbm), (ns, ns_hbm)))
    ]

    started = []

    def put(src, dst, recv_sem, to):
        copy = pltpu.make_async_remote_copy(
            src_ref=src, dst_ref=dst, send_sem=send.at[len(started)],
            recv_sem=recv_sem, device_id=to, device_id_type=MESH,
        )
        copy.start()
        started.append(copy)

    def got(dst, recv_sem):
        pltpu.make_async_remote_copy(
            src_ref=dst, dst_ref=dst, send_sem=send.at[0],
            recv_sem=recv_sem, device_id=dev(dc=1), device_id_type=MESH,
        ).wait_recv()

    def split_basis(src, base):
        @pl.loop(0, K // 16)
        def _(i):
            hi, lo = halves(src[pl.ds(pl.multiple_of(i * 16, 16), 16), :])
            at = pl.multiple_of(base + i * 16, 16)
            bhi[pl.ds(at, 16), :] = hi
            blo[pl.ds(at, 16), :] = lo

    loads[0].wait()
    for e in (0, 1):
        for j in range(4):
            gl[e, j] = grad[(yl + j) % 4, (c + e) % 2]
    g[t, 0] = gl[0]
    pl.semaphore_wait(barrier, len(friends))

    tp = ((yh + 1) % 2) * 4 + x
    HALF = (pl.ds(0, 2), pl.ds(2, 2))
    for h in (0, 1):
        for e in (0, 1):
            put(gl.at[e, HALF[h]], g.at[t, e, HALF[h]], g_sem.at[1, e, h], dev(dh=1, dc=e))
    for j in (1, 3, 2):
        for e in (0, 1):
            put(gl.at[e], g.at[t, e], g_sem.at[1 + j, e, 0], dev(dx=j, dc=e))
    put(gl.at[1], g.at[t, 1], g_sem.at[0, 1, 0], dev(dc=1))
    put(basis, sib, basis_sem, dev(dc=1))
    loads[1].wait()
    split_basis(own, 0)
    for h in (0, 1):
        for e in (0, 1):
            got(g.at[tp, e, HALF[h]], g_sem.at[1, e, h])
        for j in (1, 3, 2):
            put(
                g.at[tp, :, HALF[h]], g.at[tp, :, HALF[h]],
                g_sem.at[4 + j, 0, h], dev(dx=j),
            )
    got(sib, basis_sem)
    split_basis(sib, K)
    got(g.at[t, 1], g_sem.at[0, 1, 0])
    for j in (1, 3, 2):
        for e in (0, 1):
            got(g.at[yh * 4 + (x + 4 - j) % 4, e], g_sem.at[1 + j, e, 0])

    def split_grad(side):
        first = pl.multiple_of(side * 128, 128)
        for e in (0, 1):
            hi, lo = halves(g[pl.ds(side * 4, 4), e].reshape(128, K))
            ast[pl.ds(first, 128), e * K : (e + 1) * K] = hi
            ast[pl.ds(256 + first, 128), e * K : (e + 1) * K] = lo

    def front(base, width, side=None):
        for at in range(base, base + width, 256):
            step = min(256, base + width - at)
            cols = pl.ds(at, step)
            if side is None:
                hi, both, rows, blocks = ast[0:256, :], ast[...], 256, pl.ds(0, 8)
            else:
                first = pl.multiple_of(side * 128, 128)
                hi = ast[pl.ds(first, 128), :]
                both = jnp.concatenate([hi, ast[pl.ds(256 + first, 128), :]], 0)
                rows, blocks = 128, pl.ds(side * 4, 4)
            big = jnp.dot(both, bhi[:, cols], preferred_element_type=F32)
            out = big[0:rows] + big[rows : 2 * rows]
            out += jnp.dot(hi, blo[:, cols], preferred_element_type=F32)
            pf[blocks, :, :, cols] = out.reshape(rows // 32, 4, 8, step)

    acols = [pl.ds(*PARTS[a]) for a in (0, 1)]
    bcols = pl.ds(WA, WB)

    def front_b(side, n):
        front(WA, WB, side)
        blocks = pl.ds(side * 4, 4)
        for j in (1, 2, 3):
            put(
                pf.at[blocks, j, :, bcols], yb.at[j - 1, blocks],
                yb_sem.at[n, j - 1], dev(dl=j),
            )

    split_grad(yh)
    front_b(yh, 0)
    for h in (0, 1):
        for j in (1, 3, 2):
            got(
                g.at[((yh + 1) % 2) * 4 + (x + 4 - j) % 4, :, HALF[h]],
                g_sem.at[4 + j, 0, h],
            )
    split_grad((yh + 1) % 2)

    SIGN = (1, -1)

    def zed(k):
        return (z + k + 16) % 8

    def send_a(a, s, j, way):
        put(
            pf.at[zed(SIGN[way] * (4 - s)), j, :, acols[a]],
            ra.at[way, s, j, :, acols[a]],
            ra_sem.at[way, a, s, j], dev(dz=SIGN[way]),
        )

    def add_a(a, s, j, way):
        piece = ra.at[way, s, j, :, acols[a]]
        got(piece, ra_sem.at[way, a, s, j])
        at = zed(SIGN[way] * (3 - s))
        pf[at, j, :, acols[a]] = pf[at, j, :, acols[a]] + piece[...]

    def round_a(a, r):
        for j in (2, 3, 1, 0):
            for way in (0, 1):
                s = r if (j >= 2) == (way == 0) else r + 1
                if s >= 1 and r >= 1 and s <= 4:
                    add_a(a, s - 1, j, way)
                if s <= 3:
                    send_a(a, s, j, way)
            if r == 4 and j:
                put(
                    pf.at[z, j, :, acols[a]], ya.at[j - 1, :, acols[a]],
                    ya_sem.at[a, j - 1], dev(dl=j),
                )

    def begin_b():
        for n, side in enumerate((yh, (yh + 1) % 2)):
            for j in (1, 2, 3):
                got(yb.at[j - 1, pl.ds(side * 4, 4)], yb_sem.at[n, j - 1])
        pf[:, 0, :, bcols] = pf[:, 0, :, bcols] + yb[0] + yb[1] + yb[2]
        for i, k in enumerate(FAR):
            put(pf.at[zed(k), 0, :, bcols], rb.at[i], rb_sem.at[i], dev(dz=k))

    def end_b():
        total = pf[z, 0, :, bcols]
        for i in range(7):
            got(rb.at[i], rb_sem.at[i])
            total = total + rb[i]
        moments(total, bcols)
        block = d.at[z, 0, :, bcols]
        for i, k in enumerate(FAR):
            put(block, block, db_sem.at[i], dev(dz=k))
        spread_b(0)

    def moments(rotated, cols):
        a, b, direction = moment_step(rotated, m1[:, cols], m2[:, cols])
        nf[:, cols] = a
        ns[:, cols] = b
        d[z, 0, :, cols] = direction

    def fwd_a(a, s, j):
        for way in (0, 1):
            at = zed(-SIGN[way] * s)
            block = d.at[at, j, :, acols[a]]
            if s:
                got(block, da_sem.at[way, a, s - 1, j])
            if s < 3 or (j < 2) == (way == 0):
                put(block, block, da_sem.at[way, a, s, j], dev(dz=SIGN[way]))

    def begin_a(a):
        for j in (1, 2, 3):
            got(ya.at[j - 1, :, acols[a]], ya_sem.at[a, j - 1])
        moments(
            pf[z, 0, :, acols[a]] + ya[0, :, acols[a]] + ya[1, :, acols[a]]
            + ya[2, :, acols[a]], acols[a],
        )
        for j in (1, 2, 3):
            put(
                d.at[z, 0, :, acols[a]], d.at[z, 4 - j, :, acols[a]],
                dya_sem.at[a, j - 1], dev(dl=j),
            )
        fwd_a(a, 0, 0)

    def gather_a(a, s):
        if s:
            fwd_a(a, s, 0)
        for j in (3, 1, 2):
            if s == 0:
                got(d.at[z, j, :, acols[a]], dya_sem.at[a, 3 - j])
            fwd_a(a, s, j)

    def end_a(a):
        for j in range(4):
            got(d.at[zed(4), j, :, acols[a]], da_sem.at[j // 2, a, 3, j])

    def spread_b(k):
        for j in (1, 2, 3):
            put(
                d.at[zed(k), 0, :, bcols], d.at[zed(k), 4 - j, :, bcols],
                dyb_sem.at[k % 8, j - 1], dev(dl=j),
            )

    def gather_b(*ks):
        for k in ks:
            got(d.at[zed(k), 0, :, bcols], db_sem.at[FAR.index(4 if k == 4 else -k)])
            spread_b(k)

    def wait_b(*ks):
        for k in ks:
            for j in (1, 2, 3):
                got(d.at[zed(k), 4 - j, :, bcols], dyb_sem.at[k % 8, j - 1])

    NT = (((1,), (1,)), ((), ()))

    def product(hi, lo, cols):
        rows = hi.shape[0]
        big = lax.dot_general(
            jnp.concatenate([hi, lo], 0), bhi[:, cols], NT, preferred_element_type=F32
        )
        out = big[0:rows] + big[rows : 2 * rows]
        return out + lax.dot_general(hi, blo[:, cols], NT, preferred_element_type=F32)

    cond_sends = []

    def back(part, ks):
        width = C - PARTS[0][1] if part else PARTS[0][1]
        cols = pl.ds(part * PARTS[0][1], width)
        parts = [d[zed(k), :, :, cols].reshape(32, width) for k in ks]
        out = product(*halves(jnp.concatenate(parts, 0) if len(ks) > 1 else parts[0]), cols)
        for i, k in enumerate(ks):
            mine = out[32 * i : 32 * i + 32]
            u[zed(k)] = u[zed(k)] + mine if part else mine
        if part == 0:
            return
        for k in ks:
            tt = zed(k)
            xx, hh = tt % 4, tt // 4
            slot = jnp.minimum((xx + 7 - x) % 4, 2)
            copy = pltpu.make_async_remote_copy(
                src_ref=u.at[tt], dst_ref=xr.at[hh, slot],
                send_sem=send.at[SB + len(cond_sends)],
                recv_sem=x_sem.at[hh, slot],
                device_id=(f, yh * 4 + xx), device_id_type=MESH,
            )
            cond_sends.append((copy, xx != x))

            @pl.when(xx != x)
            def _():
                copy.start()

    other = (yh + 1) % 2

    def final_copy(i, src, to):
        return pltpu.make_async_remote_copy(
            src_ref=src, dst_ref=fin.at[i], send_sem=send.at[SB + 8 + i],
            recv_sem=fin_sem.at[i], device_id=to, device_id_type=MESH,
        )

    final = [
        final_copy(0, st.at[yh, 1], dev(dc=1)),
        final_copy(1, st.at[other, 0], dev(dh=1)),
        final_copy(2, st.at[other, 1], dev(dh=1, dc=1)),
    ]

    def finish(k):
        tt = zed(k)
        hh = tt // 4

        @pl.when(tt % 4 == x)
        def _():
            for j in (1, 2, 3):
                got(xr.at[hh, j - 1], x_sem.at[hh, j - 1])
            total = u[tt] + xr[hh, 0] + xr[hh, 1] + xr[hh, 2]
            for e in (0, 1):
                st[hh, e] = total[:, e * K : (e + 1) * K]

            @pl.when(hh == yh)
            def _():
                final[0].start()

            @pl.when(hh != yh)
            def _():
                final[1].start()
                final[2].start()

    front(*PARTS[0])
    round_a(0, 0)
    front_b((yh + 1) % 2, 1)
    front(*PARTS[1])
    round_a(1, 0)
    for copy in loads[2:]:
        copy.wait()
    round_a(0, 1)
    round_a(1, 1)
    round_a(0, 2)
    round_a(1, 2)
    round_a(0, 3)
    round_a(1, 3)
    begin_b()
    round_a(0, 4)
    round_a(1, 4)
    begin_a(0)
    begin_a(1)
    end_b()
    gather_a(0,0)
    gather_a(1,0)
    gather_a(0,1)
    gather_b(1,-1)
    gather_b(2,-2)
    gather_a(1,1)
    gather_b(3,-3)
    gather_b(4)
    back(0,[0])
    back(0,[1,-1])
    outs[1].start()
    outs[2].start()
    gather_a(0,2)
    wait_b(0)
    back(1,[0])
    gather_a(1,2)
    back(0,[2,-2])
    wait_b(1,-1)
    back(1,[1,-1])
    gather_a(0, 3)
    gather_a(1, 3)
    finish(0)
    back(0, [3, -3])
    wait_b(2, -2)
    back(1, [2, -2])
    finish(1)
    finish(-1)
    end_a(0)
    back(0, [4])
    wait_b(3, -3)
    back(1, [3, -3])
    finish(2)
    finish(-2)
    end_a(1)
    wait_b(4)
    back(1, [4])
    finish(3)
    finish(-3)
    finish(4)

    for i in range(3):
        got(fin.at[i], fin_sem.at[i])
    mine = st[yh, 0] + fin[1]
    theirs = fin[0] + fin[2]
    for j in range(4):
        update[(yl + j) % 4, c] = mine[8 * j : 8 * j + 8]
        update[(yl + j) % 4, 1 - c] = theirs[8 * j : 8 * j + 8]

    assert len(started) <= SB
    outs[0].start()
    for copy in started:
        copy.wait_send()
    for copy, pred in cond_sends:
        @pl.when(pred)
        def _():
            copy.wait_send()
    for copy in final:
        copy.wait_send()
    for copy in outs:
        copy.wait()


def hand_over(a, b, c, to_a, to_b, to_c):
    to_a[...] = a[...]
    to_b[...] = b[...]
    to_c[...] = c[...]


def shards(grad, basis, m1, m2):
    anywhere = pl.BlockSpec(memory_space=pl.ANY)
    dma = pltpu.SemaphoreType.DMA
    update, nf, ns = pl.pallas_call(
        kernel,
        out_shape=(
            jax.ShapeDtypeStruct((4, 2, 8, K), F32),
            jax.ShapeDtypeStruct((8, C), F32),
            jax.ShapeDtypeStruct((8, C), F32),
        ),
        in_specs=[anywhere] * 4,
        out_specs=(anywhere,) * 3,
        scratch_shapes=[
            pltpu.VMEM((4, 2, 8, K), F32),
            pltpu.VMEM((8, C), F32),
            pltpu.VMEM((8, C), F32),
            pltpu.VMEM((K, C), F32),
            pltpu.VMEM((K, C), F32),
            pltpu.VMEM((2 * K, C), BF16),
            pltpu.VMEM((2 * K, C), BF16),
            pltpu.VMEM((4, 2, 8, K), F32),
            pltpu.VMEM((8, C), F32),
            pltpu.VMEM((8, C), F32),
            pltpu.VMEM((2, 4, 8, K), F32),
            pltpu.VMEM((8, 2, 4, 8, K), F32),
            pltpu.VMEM((512, 2 * K), BF16),
            pltpu.VMEM((8, 4, 8, C), F32),
            pltpu.VMEM((2, 4, 4, 8, WA), F32),
            pltpu.VMEM((3, 8, WA), F32),
            pltpu.VMEM((3, 8, 8, WB), F32),
            pltpu.VMEM((7, 8, WB), F32),
            pltpu.VMEM((8, 4, 8, C), F32),
            pltpu.VMEM((8, 32, 2 * K), F32),
            pltpu.VMEM((2, 3, 32, 2 * K), F32),
            pltpu.VMEM((2, 2, 32, K), F32),
            pltpu.VMEM((3, 32, K), F32),
            dma((7,)),
            dma((SB + 11,)),
            dma,
            dma((8, 2, 2)),
            dma((2, 2, 4, 4)),
            dma((2, 3)),
            dma((2, 3)),
            dma((7,)),
            dma((2, 2, 4, 4)),
            dma((2, 3)),
            dma((7,)),
            dma((8, 3)),
            dma((2, 3)),
            dma((3,)),
        ],
        compiler_params=pltpu.CompilerParams(
            collective_id=0, has_side_effects=True, vmem_limit_bytes=58 * 2**20
        ),
        name="soap_step",
    )(grad.reshape(4, 2, 8, K), basis, m1, m2)
    update, nf, ns = pl.pallas_call(
        hand_over,
        out_shape=tuple(jax.ShapeDtypeStruct(a.shape, F32) for a in (update, nf, ns)),
        name="hand_over",
    )(update, nf, ns)
    return update.reshape(64, K), nf, ns


def solution(mesh):
    return jax.shard_map(
        shards,
        mesh=mesh,
        in_specs=(
            P("tensor", "fsdp"),
            P("fsdp", "tensor"),
            P("fsdp", "tensor"),
            P("fsdp", "tensor"),
        ),
        out_specs=(P("tensor", "fsdp"), P("fsdp", "tensor"), P("fsdp", "tensor")),
        check_vma=False,
    )
```

time: 568 us -> 88.3 us (0.16)
  waiting for transfers between devices: 493 us -> 0 us
  Pallas kernels: 0 us -> 87.2 us
  blocking collectives: 45.5 us -> 0 us
  between operations: 13.8 us -> 0.64 us
  matrix products: 11.5 us -> 0 us
    reduce_scatter x2 -> x0, waiting for transfers between devices: 358 us -> none  [the longest x1 274 us: shards(): lax.psum_scatter(partial_front, 'fsdp', scatter_dimension=0, tiled=True)]
    all_gather x1 -> x0, waiting for transfers between devices: 134 us -> none  [shards(): lax.all_gather(direction, 'fsdp', axis=0, tiled=True)]
    pallas_call x0 -> x2, Pallas kernels: none -> 87.2 us  [the longest x1 85.6 us: shards(): pl.pallas_call(kernel, out_shape=(jax.ShapeDtypeStruct((4, 2, 8, K), F32)...]
    all_gather x1 -> x0, blocking collectives: 45.5 us -> none  [shards(): lax.all_gather(grad, 'tensor', axis=0, tiled=True)]
    dot_general x2 -> x0, matrix products: 11.5 us -> none  [the longest x1 6.45 us: shards(): lax.dot_general(lax.all_gather(direction, 'fsdp', axis=0, tiled=True), ba...]
  transfers between devices with their start and end apart: 3 -> 0, of which waited for: 3 -> 0; matrix products, arithmetic and copies ran while one was open for 0% -> 0% of each run, Pallas kernels for 0% -> 0%
where the time goes in v2:
time: 88.3 us; the launch traced here: 87.8 us
  Pallas kernels  87.2 us (99%)
    pallas_call x1, Pallas kernels, shards(): pl.pallas_call(kernel, out_shape=(jax.ShapeDtypeStruct((4, 2, 8, K), F32)...  85.6 us

profile of v2, /device:TPU:56, one launch (start us, length us, event | category | flops | bytes accessed | tf_op | source)
XLA Modules:
  0.0 87.8 jit_solution(14693699390742818092)
XLA Ops:
  0.6 85.6 %soap_step.1 = (f32[4,2,8,256]{3,2,1,0:T(8,128)}, f32[8,2048]{1,0:T(8,128)}, f32[8,2048]{1,0:T(8,128)}) custom-call(f32[4,2,8,256]{3,2,1,0:T(8,128)} %bitcast.2, f32[256,2048]{1,0:T(8,128)} %basis.1, f32[8,2048]{1,0:T(8,128)} %m1_hbm.1, f32[8,2048]{1,0:T(8,128)} %m2_hbm.1), custom_call_target="tpu_custom_call" | custom-call | tf_op jit(solution)/shard_map/soap_step/pallas_call | solution.py:446
  86.2 1.6 %hand_over.1 = (f32[4,2,8,256]{3,2,1,0:T(8,128)}, f32[8,2048]{1,0:T(8,128)}, f32[8,2048]{1,0:T(8,128)}) custom-call(f32[4,2,8,256]{3,2,1,0:T(8,128)} %get-tuple-element.9.a, f32[8,2048]{1,0:T(8,128)} %get-tuple-element.10.b, f32[8,2048]{1,0:T(8,128)} %get-tuple-element.11.c), custom_call_target="tpu_custom_call" | custom-call | tf_op jit(solution)/shard_map/hand_over/pallas_call | solution.py:499

commit v3 on v2

--- a/solution.py
+++ b/solution.py
@@ -10,7 +10,7 @@
 STEP = 10
 C = 2048
 K = 256
-PARTS = ((0, 768), (768, 768))
+PARTS = ((0, 1024), (1024, 512))
 WA = PARTS[1][0] + PARTS[1][1]
 WB = C - WA
 FAR = (4, 3, -3, 2, -2, 1, -1)
@@ -163,6 +163,8 @@
 
     split_grad(yh)
     front_b(yh, 0)
+    for part in PARTS:
+        front(*part, yh)
     for h in (0, 1):
         for j in (1, 3, 2):
             got(
@@ -282,47 +284,46 @@
 
     NT = (((1,), (1,)), ((), ()))
 
-    def product(hi, lo, cols):
-        rows = hi.shape[0]
-        big = lax.dot_general(
-            jnp.concatenate([hi, lo], 0), bhi[:, cols], NT, preferred_element_type=F32
-        )
-        out = big[0:rows] + big[rows : 2 * rows]
-        return out + lax.dot_general(hi, blo[:, cols], NT, preferred_element_type=F32)
-
     cond_sends = []
 
     def back(part, ks):
-        width = C - PARTS[0][1] if part else PARTS[0][1]
-        cols = pl.ds(part * PARTS[0][1], width)
+        first, width = (PARTS[0], (PARTS[0][1], C - PARTS[0][1]), (WA, WB), PARTS[1])[part]
+        cols = pl.ds(first, width)
+        rows = 32 * len(ks)
         parts = [d[zed(k), :, :, cols].reshape(32, width) for k in ks]
-        out = product(*halves(jnp.concatenate(parts, 0) if len(ks) > 1 else parts[0]), cols)
-        for i, k in enumerate(ks):
-            mine = out[32 * i : 32 * i + 32]
-            u[zed(k)] = u[zed(k)] + mine if part else mine
-        if part == 0:
-            return
-        for k in ks:
-            tt = zed(k)
-            xx, hh = tt % 4, tt // 4
-            slot = jnp.minimum((xx + 7 - x) % 4, 2)
-            copy = pltpu.make_async_remote_copy(
-                src_ref=u.at[tt], dst_ref=xr.at[hh, slot],
-                send_sem=send.at[SB + len(cond_sends)],
-                recv_sem=x_sem.at[hh, slot],
-                device_id=(f, yh * 4 + xx), device_id_type=MESH,
-            )
-            cond_sends.append((copy, xx != x))
-
-            @pl.when(xx != x)
-            def _():
-                copy.start()
+        hi, lo = halves(jnp.concatenate(parts, 0) if len(ks) > 1 else parts[0])
+        both = jnp.concatenate([hi, lo], 0)
+        for e in (1, 0):
+            at = pl.ds(e * K, K)
+            big = lax.dot_general(both, bhi[at, cols], NT, preferred_element_type=F32)
+            out = big[0:rows] + big[rows : 2 * rows]
+            out += lax.dot_general(hi, blo[at, cols], NT, preferred_element_type=F32)
+            for i, k in enumerate(ks):
+                mine = out[32 * i : 32 * i + 32]
+                u[zed(k), e] = u[zed(k), e] + mine if part else mine
+            if part in (0, 2):
+                continue
+            for k in ks:
+                tt = zed(k)
+                xx, hh = tt % 4, tt // 4
+                slot = jnp.minimum((xx + 7 - x) % 4, 2)
+                copy = pltpu.make_async_remote_copy(
+                    src_ref=u.at[tt, e], dst_ref=xr.at[hh, slot, e],
+                    send_sem=send.at[SB + len(cond_sends)],
+                    recv_sem=x_sem.at[hh, slot, e],
+                    device_id=(f, yh * 4 + xx), device_id_type=MESH,
+                )
+                cond_sends.append((copy, xx != x))
+
+                @pl.when(xx != x)
+                def _():
+                    copy.start()
 
     other = (yh + 1) % 2
 
     def final_copy(i, src, to):
         return pltpu.make_async_remote_copy(
-            src_ref=src, dst_ref=fin.at[i], send_sem=send.at[SB + 8 + i],
+            src_ref=src, dst_ref=fin.at[i], send_sem=send.at[SB + 16 + i],
             recv_sem=fin_sem.at[i], device_id=to, device_id_type=MESH,
         )
 
@@ -338,25 +339,25 @@
 
         @pl.when(tt % 4 == x)
         def _():
-            for j in (1, 2, 3):
-                got(xr.at[hh, j - 1], x_sem.at[hh, j - 1])
-            total = u[tt] + xr[hh, 0] + xr[hh, 1] + xr[hh, 2]
-            for e in (0, 1):
-                st[hh, e] = total[:, e * K : (e + 1) * K]
-
-            @pl.when(hh == yh)
-            def _():
-                final[0].start()
-
-            @pl.when(hh != yh)
-            def _():
-                final[1].start()
-                final[2].start()
-
-    front(*PARTS[0])
+            for e in (1, 0):
+                for j in (1, 3, 2):
+                    got(xr.at[hh, j - 1, e], x_sem.at[hh, j - 1, e])
+                st[hh, e] = u[tt, e] + xr[hh, 0, e] + xr[hh, 1, e] + xr[hh, 2, e]
+                if e:
+
+                    @pl.when(hh == yh)
+                    def _():
+                        final[0].start()
+
+                @pl.when(hh != yh)
+                def _():
+                    final[1 + e].start()
+
+    late = (yh + 1) % 2
+    front(*PARTS[0], late)
     round_a(0, 0)
-    front_b((yh + 1) % 2, 1)
-    front(*PARTS[1])
+    front_b(late, 1)
+    front(*PARTS[1], late)
     round_a(1, 0)
     for copy in loads[2:]:
         copy.wait()
@@ -405,9 +406,10 @@
     back(1, [3, -3])
     finish(2)
     finish(-2)
+    wait_b(4)
+    back(2, [4])
     end_a(1)
-    wait_b(4)
-    back(1, [4])
+    back(3, [4])
     finish(3)
     finish(-3)
     finish(4)
@@ -472,12 +474,12 @@
             pltpu.VMEM((3, 8, 8, WB), F32),
             pltpu.VMEM((7, 8, WB), F32),
             pltpu.VMEM((8, 4, 8, C), F32),
-            pltpu.VMEM((8, 32, 2 * K), F32),
-            pltpu.VMEM((2, 3, 32, 2 * K), F32),
+            pltpu.VMEM((8, 2, 32, K), F32),
+            pltpu.VMEM((2, 3, 2, 32, K), F32),
             pltpu.VMEM((2, 2, 32, K), F32),
             pltpu.VMEM((3, 32, K), F32),
             dma((7,)),
-            dma((SB + 11,)),
+            dma((SB + 19,)),
             dma,
             dma((8, 2, 2)),
             dma((2, 2, 4, 4)),
@@ -488,7 +490,7 @@
             dma((2, 3)),
             dma((7,)),
             dma((8, 3)),
-            dma((2, 3)),
+            dma((2, 3, 2)),
             dma((3,)),
         ],
         compiler_params=pltpu.CompilerParams(

time: 88.3 us -> 87.4 us (0.990)
  no operation moved by 1% of the time
where the time goes in v3:
time: 87.4 us; the launch traced here: 87.2 us
  Pallas kernels  86.5 us (99%)
    pallas_call x1, Pallas kernels, shards(): pl.pallas_call(kernel, out_shape=(jax.ShapeDtypeStruct((4, 2, 8, K), F32)...  85 us

profile of v3, /device:TPU:56, one launch (start us, length us, event | category | flops | bytes accessed | tf_op | source)
XLA Modules:
  0.0 87.2 jit_solution(11688117995426884707)
XLA Ops:
  0.6 85.0 %soap_step.1 = (f32[4,2,8,256]{3,2,1,0:T(8,128)}, f32[8,2048]{1,0:T(8,128)}, f32[8,2048]{1,0:T(8,128)}) custom-call(f32[4,2,8,256]{3,2,1,0:T(8,128)} %bitcast.2, f32[256,2048]{1,0:T(8,128)} %basis.1, f32[8,2048]{1,0:T(8,128)} %m1_hbm.1, f32[8,2048]{1,0:T(8,128)} %m2_hbm.1), custom_call_target="tpu_custom_call" | custom-call | tf_op jit(solution)/shard_map/soap_step/pallas_call | solution.py:448
  85.6 1.6 %hand_over.1 = (f32[4,2,8,256]{3,2,1,0:T(8,128)}, f32[8,2048]{1,0:T(8,128)}, f32[8,2048]{1,0:T(8,128)}) custom-call(f32[4,2,8,256]{3,2,1,0:T(8,128)} %get-tuple-element.9.a, f32[8,2048]{1,0:T(8,128)} %get-tuple-element.10.b, f32[8,2048]{1,0:T(8,128)} %get-tuple-element.11.c), custom_call_target="tpu_custom_call" | custom-call | tf_op jit(solution)/shard_map/hand_over/pallas_call | solution.py:501

commit v4 on v3

--- a/solution.py
+++ b/solution.py
@@ -371,33 +371,33 @@
     round_a(0, 4)
     round_a(1, 4)
     begin_a(0)
+    end_b()
     begin_a(1)
-    end_b()
-    gather_a(0,0)
-    gather_a(1,0)
-    gather_a(0,1)
-    gather_b(1,-1)
-    gather_b(2,-2)
-    gather_a(1,1)
-    gather_b(3,-3)
+    gather_a(0, 0)
+    gather_a(1, 0)
+    back(0, [0])
+    gather_a(0, 1)
+    gather_b(1, -1)
+    gather_b(2, -2)
+    gather_a(1, 1)
+    gather_b(3, -3)
     gather_b(4)
-    back(0,[0])
-    back(0,[1,-1])
+    back(0, [1, -1])
     outs[1].start()
     outs[2].start()
-    gather_a(0,2)
+    gather_a(0, 2)
     wait_b(0)
-    back(1,[0])
-    gather_a(1,2)
-    back(0,[2,-2])
-    wait_b(1,-1)
-    back(1,[1,-1])
+    back(1, [0])
+    back(0, [2, -2])
+    gather_a(1, 2)
+    wait_b(1, -1)
+    back(1, [1, -1])
     gather_a(0, 3)
-    gather_a(1, 3)
-    finish(0)
     back(0, [3, -3])
     wait_b(2, -2)
     back(1, [2, -2])
+    gather_a(1, 3)
+    finish(0)
     finish(1)
     finish(-1)
     end_a(0)

time: 87.4 us -> 85.6 us (0.979)
  Pallas kernels: 86.5 us -> 84.8 us
    pallas_call x1, Pallas kernels: 85 us -> 83.2 us  [shards(): pl.pallas_call(kernel, out_shape=(jax.ShapeDtypeStruct((4, 2, 8, K), F32)...]
where the time goes in v4:
time: 85.6 us; the launch traced here: 85.4 us
  Pallas kernels  84.8 us (99%)
    pallas_call x1, Pallas kernels, shards(): pl.pallas_call(kernel, out_shape=(jax.ShapeDtypeStruct((4, 2, 8, K), F32)...  83.2 us

profile of v4, /device:TPU:56, one launch (start us, length us, event | category | flops | bytes accessed | tf_op | source)
XLA Modules:
  0.0 85.4 jit_solution(2248013577905913517)
XLA Ops:
  0.6 83.2 %soap_step.1 = (f32[4,2,8,256]{3,2,1,0:T(8,128)}, f32[8,2048]{1,0:T(8,128)}, f32[8,2048]{1,0:T(8,128)}) custom-call(f32[4,2,8,256]{3,2,1,0:T(8,128)} %bitcast.2, f32[256,2048]{1,0:T(8,128)} %basis.1, f32[8,2048]{1,0:T(8,128)} %m1_hbm.1, f32[8,2048]{1,0:T(8,128)} %m2_hbm.1), custom_call_target="tpu_custom_call" | custom-call | tf_op jit(solution)/shard_map/soap_step/pallas_call | solution.py:448
  83.9 1.6 %hand_over.1 = (f32[4,2,8,256]{3,2,1,0:T(8,128)}, f32[8,2048]{1,0:T(8,128)}, f32[8,2048]{1,0:T(8,128)}) custom-call(f32[4,2,8,256]{3,2,1,0:T(8,128)} %get-tuple-element.9.a, f32[8,2048]{1,0:T(8,128)} %get-tuple-element.10.b, f32[8,2048]{1,0:T(8,128)} %get-tuple-element.11.c), custom_call_target="tpu_custom_call" | custom-call | tf_op jit(solution)/shard_map/hand_over/pallas_call | solution.py:501
